TPU v7x, 512 devices: a whole 4x8x8 slice. The times are simulated.
512 devices in a mesh: wide: 64 (over y_hi, z, core), narrow: 8 (over y_lo, x).
Axes of the slice: x: 4, y: 8 (y_hi: 4, y_lo: 2; y = y_hi * 2 + y_lo), z: 8, core: 2. Of those that a mesh axis runs over, the one named last changes fastest.
Arguments:
- tokens: bfloat16 [262144, 768], P(('wide', 'narrow')), may hold values from -28 to 28
- proj_weight: bfloat16 [768, 2304], P('narrow'), may hold values from -0.375 to 0.375
- out_weight: bfloat16 [768, 768], P('narrow'), may hold values from -0.21875 to 0.21875
Outputs:
- mixed: bfloat16 [262144, 768], P(('wide', 'narrow'))
All inputs are finite; a program needn't handle non-finite values.
Results may differ from a plain program's by a relative error of at most 0.012.
The roundings to bfloat16 on the way count: a program that leaves them out, or rounds other values in their place, can miss the bound.
Values may be sent and summed in bfloat16 or wider, within the bound.
A program may use at most 64 MiB of HBM per device.

v0:
```python
import jax
import jax.numpy as jnp
from jax import lax
from jax.sharding import PartitionSpec as P

HEAD_COUNT = 12
HEAD_WIDTH = 64
SPACING_LEVEL1 = 4
SPACING_LEVEL2 = 16
SPACING_LEVEL3 = 256


score_scale = 0.125


def pick_rows(values_in, stride, start_index):
    count, heads_n, span_width = values_in.shape
    grouped = values_in.reshape(count // stride, stride, heads_n, span_width)
    chosen = jnp.arange(stride)[:, None] == start_index[None, :]
    return jnp.sum(
        jnp.where(chosen[None, :, :, None], grouped, jnp.zeros((), values_in.dtype)), axis=1
    )


def scatter_rows(values_in, stride, start_index, background):
    count, heads_n, span_width = values_in.shape
    grouped = background.reshape(count, stride, heads_n, span_width)
    chosen = jnp.arange(stride)[:, None] == start_index[None, :]
    return jnp.where(chosen[None, :, :, None], values_in[:, None], grouped).reshape(
        background.shape
    )


def level_terms(queries, keys, values_in):
    scores = (
        jnp.einsum("qhe,khe->hqk", queries, keys, preferred_element_type=jnp.float32) * score_scale
    )
    peak = jnp.max(scores, axis=-1, keepdims=True)
    weights = jnp.exp(scores - peak)
    totals = jnp.sum(weights, axis=-1, keepdims=True)
    numerator = jnp.einsum(
        "hqk,khe->qhe", weights.astype(jnp.bfloat16), values_in, preferred_element_type=jnp.float32
    )
    return (jnp.transpose(peak, (1, 0, 2)), jnp.transpose(totals, (1, 0, 2)), numerator)


def combine(first, central_level, distant_level, head_index):
    start_index = head_index // SPACING_LEVEL1
    maximum_first, sum_first, weighted_first = first
    maximum_second = scatter_rows(
        central_level[0], SPACING_LEVEL2 // SPACING_LEVEL1, start_index, maximum_first
    )
    sum_second = scatter_rows(
        central_level[1], SPACING_LEVEL2 // SPACING_LEVEL1, start_index, jnp.zeros_like(sum_first)
    )
    weighted_second = scatter_rows(
        central_level[2],
        SPACING_LEVEL2 // SPACING_LEVEL1,
        start_index,
        jnp.zeros_like(weighted_first),
    )
    maximum_third = scatter_rows(
        distant_level[0], SPACING_LEVEL3 // SPACING_LEVEL1, start_index, maximum_first
    )
    sum_third = scatter_rows(
        distant_level[1], SPACING_LEVEL3 // SPACING_LEVEL1, start_index, jnp.zeros_like(sum_first)
    )
    weighted_third = scatter_rows(
        distant_level[2],
        SPACING_LEVEL3 // SPACING_LEVEL1,
        start_index,
        jnp.zeros_like(weighted_first),
    )
    highest = jnp.maximum(maximum_first, jnp.maximum(maximum_second, maximum_third))
    scale_one = jnp.exp(maximum_first - highest)
    scale_two = jnp.exp(maximum_second - highest)
    scale_three = jnp.exp(maximum_third - highest)
    totals = sum_first * scale_one + sum_second * scale_two + sum_third * scale_three
    numerator = (
        weighted_first * scale_one + weighted_second * scale_two + weighted_third * scale_three
    )
    return (numerator / totals).astype(jnp.bfloat16)


def shards(tokens, proj_weight, out_weight):
    local_rows = tokens.shape[0]
    span_width = tokens.shape[1]
    columns = tokens
    projected = jnp.dot(
        columns,
        lax.all_gather(proj_weight, "narrow", axis=0, tiled=True),
        preferred_element_type=jnp.float32,
    )
    query_matrix = (
        projected[:, :span_width].astype(jnp.bfloat16).reshape(local_rows, HEAD_COUNT, HEAD_WIDTH)
    )
    key = (
        projected[:, span_width : 2 * span_width]
        .astype(jnp.bfloat16)
        .reshape(local_rows, HEAD_COUNT, HEAD_WIDTH)
    )
    value_matrix = (
        projected[:, 2 * span_width :]
        .astype(jnp.bfloat16)
        .reshape(local_rows, HEAD_COUNT, HEAD_WIDTH)
    )
    head_index = jnp.arange(HEAD_COUNT)
    query_first = pick_rows(query_matrix, SPACING_LEVEL1, head_index % SPACING_LEVEL1)
    key_first = pick_rows(key, SPACING_LEVEL1, head_index % SPACING_LEVEL1)
    value_first = pick_rows(value_matrix, SPACING_LEVEL1, head_index % SPACING_LEVEL1)
    first = level_terms(query_first, key_first, value_first)
    query_second = pick_rows(
        query_first, SPACING_LEVEL2 // SPACING_LEVEL1, head_index // SPACING_LEVEL1
    )
    key_second = pick_rows(
        key_first, SPACING_LEVEL2 // SPACING_LEVEL1, head_index // SPACING_LEVEL1
    ).reshape(-1, span_width)
    value_second = pick_rows(
        value_first, SPACING_LEVEL2 // SPACING_LEVEL1, head_index // SPACING_LEVEL1
    ).reshape(-1, span_width)
    group_keys, group_values = (
        lax.all_gather(key_second, "narrow", axis=0, tiled=True),
        lax.all_gather(value_second, "narrow", axis=0, tiled=True),
    )
    central_level = level_terms(
        query_second,
        group_keys.reshape(-1, HEAD_COUNT, HEAD_WIDTH),
        group_values.reshape(-1, HEAD_COUNT, HEAD_WIDTH),
    )
    query_third = pick_rows(
        query_first, SPACING_LEVEL3 // SPACING_LEVEL1, head_index // SPACING_LEVEL1
    )
    key_third = pick_rows(
        key_first, SPACING_LEVEL3 // SPACING_LEVEL1, head_index // SPACING_LEVEL1
    ).reshape(-1, span_width)
    value_third = pick_rows(
        value_first, SPACING_LEVEL3 // SPACING_LEVEL1, head_index // SPACING_LEVEL1
    ).reshape(-1, span_width)
    all_keys, all_values = (
        lax.all_gather(key_third, ("wide", "narrow"), axis=0, tiled=True),
        lax.all_gather(value_third, ("wide", "narrow"), axis=0, tiled=True),
    )
    distant_level = level_terms(
        query_third,
        all_keys.reshape(-1, HEAD_COUNT, HEAD_WIDTH),
        all_values.reshape(-1, HEAD_COUNT, HEAD_WIDTH),
    )
    attended_first = combine(first, central_level, distant_level, head_index)
    attended_rows = scatter_rows(
        attended_first,
        SPACING_LEVEL1,
        head_index % SPACING_LEVEL1,
        jnp.zeros((local_rows, HEAD_COUNT, HEAD_WIDTH), jnp.bfloat16),
    ).reshape(local_rows, span_width)
    columns = attended_rows
    mixed = jnp.dot(
        columns,
        lax.all_gather(out_weight, "narrow", axis=0, tiled=True),
        preferred_element_type=jnp.float32,
    )
    return mixed.astype(jnp.bfloat16)


def solution(mesh):
    return jax.shard_map(
        shards,
        mesh=mesh,
        in_specs=(P(("wide", "narrow"), None), P("narrow", None), P("narrow", None)),
        out_specs=P(("wide", "narrow"), None),
        check_vma=False,
    )
```

profile of v0, /device:TPU:1, one launch (start us, length us, event | category | flops | bytes accessed | tf_op | source)
XLA Modules:
  0.0 2234.1 jit_solution(7556606767675142070)
XLA Ops:
  6.5 0.7 all-gather.7.cloned.1.call-update
  7.4 59.3 %all-gather.7.cloned.1.call-done = bf16[768,2304]{1,0:T(8,128)(2,1)} async-done(((bf16[96,2304]{1,0:T(8,128)(2,1)}), bf16[768,2304]{1,0:T(8,128)(2,1)}) %all-gather.7.cloned.1.call-update) | async-done | bytes 3538960 | tf_op jit(solution)/shard_map/all_gather | solution.py:91
  66.7 4.0 convolution_convert_fusion
  70.7 1.5 fusion.37
  72.2 2.7 reshape_reshape.10
  75.0 3.8 reshape_reshape.11
  78.7 3.8 reshape_reshape.12
  82.5 5.0 select_reduce_fusion
  87.5 0.8 copy-done.1
  88.3 0.6 fusion.19
  88.9 0.7 reshape.252
  89.7 0.7 reshape.254
  90.4 0.5 all-gather.9.cloned.1.call-update
  91.2 0.1 copy.70
  91.5 1.2 copy.85
  92.7 1.1 copy.71
  93.8 0.1 copy.72
  94.0 1.8 select_reduce_fusion.4
  95.8 0.1 reshape.238
  95.9 22.7 %all_gather.19 = bf16[256,768]{1,0:T(8,128)(2,1)S(1)} all-gather(bf16[32,768]{1,0:T(8,128)(2,1)S(1)} %reshape.238), channel_id=1, replica_groups=mesh['wide'=64,'narrow'=8] {'narrow'}, dimensions={0}, use_global_device_ids=true | all-gather | bytes 442368 | tf_op jit(solution)/shard_map/all_gather | solution.py:122
  118.6 0.2 copy.74
  118.9 0.1 reshape.245
  119.0 23.3 %all_gather.21 = bf16[256,768]{1,0:T(8,128)(2,1)S(1)} all-gather(bf16[32,768]{1,0:T(8,128)(2,1)S(1)} %reshape.245), channel_id=1, replica_groups=mesh['wide'=64,'narrow'=8] {'narrow'}, dimensions={0}, use_global_device_ids=true | all-gather | bytes 442368 | tf_op jit(solution)/shard_map/all_gather | solution.py:123
  142.3 0.2 copy.87
  142.5 0.3 fusion.39
  142.8 0.3 convolution_bitcast_fusion.1
  143.1 0.2 fusion.22
  143.7 0.2 broadcast_in_dim.302
  143.8 1.0 copy.88
  144.8 0.4 fusion.40
  145.2 0.1 fusion.15
  145.3 991.7 %all-gather.11.cloned.1.call-done = bf16[512,2,768]{2,1,0:T(2,128)(2,1)} async-done(((bf16[1,2,768]{2,1,0:T(2,128)(2,1)}), bf16[512,2,768]{2,1,0:T(2,128)(2,1)}) %all-gather.11.cloned.1.call-update) | async-done | bytes 1572880 | tf_op jit(solution)/shard_map/all_gather | solution.py:140
  1137.0 6.8 reshape.243
  1143.8 3.9 fusion.38
  1147.8 0.2 fusion.26
  1148.1 0.1 copy.97
  1148.6 1036.2 %all-gather.13.cloned.1.call-done = bf16[512,2,768]{2,1,0:T(2,128)(2,1)} async-done(((bf16[1,2,768]{2,1,0:T(2,128)(2,1)}), bf16[512,2,768]{2,1,0:T(2,128)(2,1)}) %all-gather.13.cloned.1.call-update) | async-done | bytes 1572880 | tf_op jit(solution)/shard_map/all_gather | solution.py:141
  2184.8 6.8 reshape.250
  2191.5 3.9 fusion.12
  2195.4 0.2 copy.92
  2195.6 1.0 broadcast_in_dim.306
  2196.6 0.4 broadcast_in_dim.307
  2197.1 1.3 fusion.8
  2198.4 0.4 copy.98
  2198.8 0.2 broadcast_select_fusion
  2199.0 2.0 select_n.168
  2201.0 23.4 %all-gather.9.cloned.1.call-done = bf16[768,768]{1,0:T(8,128)(2,1)} async-done(((bf16[96,768]{1,0:T(8,128)(2,1)}), bf16[768,768]{1,0:T(8,128)(2,1)}) %all-gather.9.cloned.1.call-update) | async-done | bytes 1179664 | tf_op jit(solution)/shard_map/all_gather | solution.py:158
  2224.4 3.2 convolution_convert_fusion.1
  (40 shorter events, 1.8 us)
Async XLA Ops:
  6.5 60.2 %copy-start = (bf16[512,768]{1,0:T(8,128)(2,1)S(1)}, bf16[512,768]{1,0:T(8,128)(2,1)}, u32[]{:S(2)}) copy-start(bf16[512,768]{1,0:T(8,128)(2,1)} %param.3) | copy-start | bytes 2359300
  6.5 60.2 %all-gather.7.cloned.1.call-start = ((), (), s32[]{:S(2)}) async-start(), calls=%async_computation | async-start | bytes 3981312 | tf_op jit(solution)/shard_map/all_gather | solution.py:91
  7.3 1129.7 %all-gather.11.cloned.1.call-start = ((), (), s32[]{:S(2)}) async-start(), calls=%async_computation.2 | async-start | bytes 1575936 | tf_op jit(solution)/shard_map/all_gather | solution.py:140
  87.5 0.8 copy-start.1
  87.5 1.4 copy-start.2
  89.6 2095.1 %all-gather.13.cloned.1.call-start = ((), (), s32[]{:S(2)}) async-start(), calls=%async_computation.3 | async-start | bytes 1575936 | tf_op jit(solution)/shard_map/all_gather | solution.py:141
  90.4 2134.0 %all-gather.9.cloned.1.call-start = ((), (), s32[]{:S(2)}) async-start(), calls=%async_computation.1 | async-start | bytes 1327104 | tf_op jit(solution)/shard_map/all_gather | solution.py:158
Sparse Core Ops, SparseCore 0:
  9.4 57.2 all-gather.6
  89.7 1047.2 all-gather.10
  1139.2 1045.5 all-gather.12
  2186.7 37.6 all-gather.8
where the time goes:
time: 2240 us; the launch traced here: 2230 us
  waiting for transfers between devices  2110 us (94%)
  blocking collectives  46 us (2%)
  local copies, waits for them, and re-layouts  37.2 us (2%)
    all_gather x1, waiting for transfers between devices, shards(): lax.all_gather(value_third, ('wide', 'narrow'), axis=0, tiled=True)  1040 us
    all_gather x1, waiting for transfers between devices, shards(): lax.all_gather(key_third, ('wide', 'narrow'), axis=0, tiled=True)  992 us
    all_gather x1, waiting for transfers between devices, shards(): lax.all_gather(proj_weight, 'narrow', axis=0, tiled=True)  59.3 us
  transfers between devices with their start and end apart: 4, of which 4 were waited for; matrix products, arithmetic and copies ran while one was open for 2% of the time, Pallas kernels for 0%

commit v1 on v0

v1 whole, which is shorter than its diff:
```python
import jax
import jax.numpy as jnp
from jax import lax
from jax.experimental import pallas as pl
from jax.experimental.pallas import tpu as pltpu
from jax.sharding import PartitionSpec as P

MESH = pl.DeviceIdType.MESH
BF = jnp.bfloat16
F32 = jnp.float32
SCALE = 0.125
LOW = -1e30


def iota(shape, dim):
    return lax.broadcasted_iota(jnp.int32, shape, dim)


def tile_of_row(r):
    j = r % 32
    s = jnp.where(j == 1, 16, jnp.where((j >= 2) & (j <= 16), j - 1, j))
    return 16 * s + 4 * ((r // 32) % 4) + r // 128


def dot(a, b):
    return jnp.dot(a, b, preferred_element_type=F32)


def dot_t(a, b):
    return lax.dot_general(a, b, (((1,), (1,)), ((), ())), preferred_element_type=F32)


def soft(q, k, v, mask=None):
    s = dot_t(q, k) * SCALE
    if mask is not None:
        s = jnp.where(mask, s, LOW)
    peak = jnp.max(s, axis=-1, keepdims=True)
    w = jnp.exp(s - peak)
    return peak, jnp.sum(w, axis=-1, keepdims=True), dot(w.astype(BF), v)


def merge(a, b):
    top = jnp.maximum(a[0], b[0])
    ea, eb = jnp.exp(a[0] - top), jnp.exp(b[0] - top)
    return top, a[1] * ea + b[1] * eb, a[2] * ea + b[2] * eb


def kernel(
    tok_hbm, wp_hbm, wo_hbm, out_ref,
    tok, perm, back, xp, wp, wo, qkv, kv2, kv3, q3, part_out, part_in, att, y,
    loc_sem, ws, wr, os_, or_, s2, r2, s3, r3,
):
    w, n = lax.axis_index("wide"), lax.axis_index("narrow")
    x, yl, core, z, yh = n % 4, n // 4, w % 2, (w // 2) % 8, w // 16
    yy = 2 * yh + yl

    def dev(dx=0, dy=0, dz=0, dc=0):
        y_ = (yy + dy) % 8
        return ((y_ // 2) * 16 + ((z + dz) % 8) * 2 + (core + dc) % 2, (y_ % 2) * 4 + (x + dx) % 4)

    def narrow_dev(k):
        return (w, (n + k) % 8)

    barrier = pltpu.get_barrier_semaphore()
    partners = (
        [dev(dx=k) for k in (1, 2, 3)] + [dev(dy=k) for k in range(1, 8)] + [dev(dz=k) for k in range(1, 8)] + [dev(dc=1)]
    )
    diag = [(w, (1 - yl) * 4 + (x + k) % 4) for k in (1, 2, 3)]
    partners = partners + diag
    for p in partners:
        pl.semaphore_signal(barrier, inc=1, device_id=p, device_id_type=MESH)

    def send(src, dst, ss, rs, to):
        c = pltpu.make_async_remote_copy(
            src_ref=src, dst_ref=dst, send_sem=ss, recv_sem=rs, device_id=to, device_id_type=MESH
        )
        c.start()
        return c

    mine = pl.ds(pl.multiple_of(96 * n, 32), 96)
    loc = [
        pltpu.make_async_copy(tok_hbm, tok, loc_sem.at[0]),
        pltpu.make_async_copy(wp_hbm, wp.at[mine], loc_sem.at[1]),
        pltpu.make_async_copy(wo_hbm, wo.at[mine], loc_sem.at[2]),
    ]
    for c in loc:
        c.start()
    pl.semaphore_wait(barrier, len(partners))

    class Gather:
        def __init__(self, src, buf, cuts, ss, rs):
            self.src, self.buf, self.ss, self.rs = src, buf, ss, rs
            q = [pl.ds(a, b - a) for a, b in zip(cuts, cuts[1:])]
            self.q = q
            self.left, self.right, self.full = pl.ds(0, cuts[2]), pl.ds(cuts[2], cuts[4] - cuts[2]), pl.ds(0, cuts[4])
            self.sent, self.passed = [], []
            self.k = 0

        def at(self, dx, other, cols):
            half = (1 - yl) if other else yl
            j = half * 4 + (x + dx) % 4
            return self.buf.at[pl.ds(pl.multiple_of(96 * j + 48 * core, 16), 48), cols]

        def go(self, src, dst, to):
            c = send(src, dst, self.ss.at[self.k], self.rs.at[self.k], to)
            self.k += 1
            self.sent.append(c)
            return c

        def twin(self, *refs):
            for ref in refs:
                self.passed.append(self.go(ref, ref, dev(dc=1)))

        def relay(self, wait, ref):
            wait.wait_recv()
            self.twin(ref)

        def phase_a(self):
            def own(cols, to):
                src = self.src.at[pl.ds(pl.multiple_of(48 * core, 16), 48), cols]
                return self.go(src, self.at(0, False, cols), to)

            self.a = [
                own(self.full, dev(dx=1)), own(self.full, dev(dx=3)), own(self.left, dev(dy=1)), own(self.right, dev(dy=7))
            ]

        def phase_b(self):
            a = self.a
            a[0].wait_recv()
            b1 = self.go(self.at(3, False, self.left), self.at(3, False, self.left), dev(dx=1))
            b3 = self.go(self.at(3, False, self.full), self.at(3, False, self.full), dev(dy=1))
            a[1].wait_recv()
            b2 = self.go(self.at(1, False, self.right), self.at(1, False, self.right), dev(dx=3))
            b4 = self.go(self.at(1, False, self.full), self.at(1, False, self.full), dev(dy=7))
            self.b = [b1, b2, b3, b4]
            self.twin(self.at(3, False, self.full), self.at(1, False, self.full))
            self.relay(a[2], self.at(0, True, self.left))
            self.relay(a[3], self.at(0, True, self.right))

        def phase_c(self):
            b1, b2, b3, b4 = self.b
            q = self.q
            b1.wait_recv()
            c3 = self.go(self.at(2, False, q[0]), self.at(2, False, q[0]), dev(dy=1))
            b2.wait_recv()
            c4 = self.go(self.at(2, False, q[3]), self.at(2, False, q[3]), dev(dy=7))
            b3.wait_recv()
            c1 = self.go(self.at(3, True, q[1]), self.at(3, True, q[1]), dev(dx=1))
            b4.wait_recv()
            c2 = self.go(self.at(1, True, q[2]), self.at(1, True, q[2]), dev(dx=3))
            self.c = [c1, c2, c3, c4]
            self.twin(self.at(2, False, self.full), self.at(3, True, self.full), self.at(1, True, self.full))

        def finish(self):
            for c, k in zip(self.c, (1, 2, 0, 3)):
                self.relay(c, self.at(2, True, self.q[k]))
            for c in self.passed:
                c.wait_recv()
            for c in self.sent:
                c.wait_send()

    proj = Gather(wp_hbm, wp, (0, 512, 1152, 1792, 2304), ws, wr)
    outp = Gather(wo_hbm, wo, (0, 256, 384, 512, 768), os_, or_)
    proj.phase_a()

    perm[...] = jnp.where(iota((512, 512), 1) == tile_of_row(iota((512, 512), 0)), 1.0, 0.0).astype(BF)
    back[...] = jnp.where(iota((512, 512), 0) == tile_of_row(iota((512, 512), 1)), 1.0, 0.0).astype(BF)
    proj.phase_b()
    loc[0].wait()
    xp[...] = dot(perm[...], tok[...]).astype(BF)
    proj.phase_c()
    outp.phase_a()
    loc[1].wait()
    proj.finish()

    for cp in range(2):
        cols = [768 * m + 128 * (2 * t + cp) for m in range(3) for t in range(3)]
        wc = jnp.concatenate([wp[:, c : c + 128] for c in cols], axis=1)
        qkv[256 * cp : 256 * cp + 256, :] = dot(xp[256 * cp : 256 * cp + 256, :], wc).astype(BF)

    low = iota((1, 128), 1) < 64
    row16 = iota((16, 128), 0)

    def second(m, cp, t):
        a = 256 * cp + 32 * t
        c = 384 * m + 128 * t
        return jnp.where(low, qkv[a : a + 32, c : c + 128].astype(F32), qkv[a + 128 : a + 160, c : c + 128].astype(F32))

    zeros8 = jnp.zeros((8, 128), F32)
    third = [jnp.zeros((16, 128), F32) for _ in range(3)]
    for m in range(3):
        for cp in range(2):
            for t in range(3):
                v = second(m, cp, t)
                i = 2 * t + cp
                if m > 0:
                    kv2[m - 1, pl.ds(pl.multiple_of(32 * n, 32), 32), 128 * i : 128 * i + 128] = v.astype(BF)
                e = jnp.concatenate([v[:8], zeros8], axis=0)
                if i:
                    e = pltpu.roll(e, 2 * i, 0)
                third[m] = jnp.where((row16 >= 2 * i) & (row16 < 2 * i + 2), e, third[m])
    q3[z] = third[0].astype(BF)
    for m in range(2):
        kv3[m, core, x, yy] = third[m + 1].astype(BF)

    sent = []
    k3 = 0

    def go3(src, dst, to):
        nonlocal k3
        c = send(src, dst, s3.at[k3], r3.at[k3], to)
        k3 += 1
        sent.append(c)
        return c

    own3 = kv3.at[:, core, x, yy]
    a3 = [go3(own3, own3, dev(dy=k)) for k in range(1, 8)]
    sq = [go3(q3.at[z], q3.at[z], dev(dz=k)) for k in range(1, 8)]
    own2 = kv2.at[:, pl.ds(pl.multiple_of(32 * n, 32), 32)]
    to2 = [dev(dx=1), dev(dx=3), dev(dx=2), (w, (1 - yl) * 4 + x)] + diag
    g2 = [send(own2, own2, s2.at[k], r2.at[k], p) for k, p in enumerate(to2)]
    sent += g2

    first = {}

    def level1(cp, t):
        for lo in range(2):
            r = slice(256 * cp + 128 * lo, 256 * cp + 128 * lo + 128)
            lanes = low if lo == 0 else ~low
            q = jnp.where(lanes, qkv[r, 128 * t : 128 * t + 128].astype(F32), 0.0).astype(BF)
            pk, tot, num = soft(q, qkv[r, 384 + 128 * t : 512 + 128 * t], qkv[r, 768 + 128 * t : 896 + 128 * t])
            att[r, 128 * t : 128 * t + 128] = jnp.where(lanes, num / tot, 0.0).astype(BF)
            b = slice(32 * t, 32 * t + 32)
            first[cp, t, lo] = pk[b], tot[b], num[b]

    for t in range(3):
        level1(0, t)
    for c in a3:
        c.wait_recv()
    plane = kv3.at[:, core, x]
    b3 = [go3(plane, plane, dev(dx=k)) for k in (1, 3, 2)]
    for t in range(3):
        level1(1, t)
    outp.phase_b()
    for c in b3:
        c.wait_recv()
    half = kv3.at[:, core]
    c3 = go3(half, half, dev(dc=1))
    outp.phase_c()
    for c in sq:
        c.wait_recv()
    c3.wait_recv()

    qa = q3[...].reshape(128, 128).astype(F32)
    qs = jnp.concatenate([jnp.where(low, qa, 0.0), jnp.where(low, 0.0, qa)], axis=0).astype(BF)
    same = (iota((256, 1024), 0) % 16) // 2 == (iota((256, 1024), 1) % 16) // 2
    pk, tot, num = soft(qs, kv3[0].reshape(1024, 128), kv3[1].reshape(1024, 128), same)
    num = jnp.where(low, num[:128], num[128:]).reshape(8, 16, 128)
    row, lane = iota((8, 16, 128), 1), iota((8, 16, 128), 2)

    def to_lanes(v):
        a, b = v[:128].reshape(8, 16, 1), v[128:].reshape(8, 16, 1)
        u = jnp.where(lane == row, a, jnp.where(lane == row + 64, b, 0.0))
        return jnp.sum(u, axis=1, keepdims=True)

    part_out[...] = jnp.where(row < 12, num, jnp.where(row == 12, to_lanes(pk), to_lanes(tot)))
    sp = [go3(part_out.at[(z + k) % 8], part_in.at[z], dev(dz=k)) for k in range(1, 8)]
    part_in[z] = part_out[z]

    for c in g2:
        c.wait_recv()
    both = {}
    for cp in range(2):
        for t in range(3):
            i = 2 * t + cp
            v = second(0, cp, t)
            q = jnp.concatenate([jnp.where(low, v, 0.0), jnp.where(low, 0.0, v)], axis=0).astype(BF)
            pk, tot, num = soft(q, kv2[0, :, 128 * i : 128 * i + 128], kv2[1, :, 128 * i : 128 * i + 128])
            for lo in range(2):
                b = slice(32 * lo, 32 * lo + 32)
                both[cp, t, lo] = merge(first[cp, t, lo], (pk[b], tot[b], num[b]))

    outp.finish()
    loc[2].wait()
    for c in sp:
        c.wait_recv()
    p = part_in[...]

    def from_lanes(v):
        a = jnp.sum(jnp.where(lane == row, v, 0.0), axis=-1, keepdims=True)
        b = jnp.sum(jnp.where(lane == row + 64, v, 0.0), axis=-1, keepdims=True)
        return jnp.where(lane < 64, a, b)

    pk, tot = from_lanes(p[:, 12:13]), from_lanes(p[:, 13:14])
    top = jnp.max(pk, axis=0)
    e = jnp.exp(pk - top[None])
    dist = (top, jnp.sum(tot * e, axis=0), jnp.sum(p * e, axis=0))

    use = iota((8, 128), 0) < 2
    for cp in range(2):
        for t in range(3):
            i = 2 * t + cp
            d = [pltpu.roll(v, 16 - 2 * i, 0)[:8] if i else v[:8] for v in dist]
            d = (jnp.where(use, d[0], LOW), jnp.where(use, d[1], 0.0), jnp.where(use, d[2], 0.0))
            for lo in range(2):
                lanes = low if lo == 0 else ~low
                pk, tot, num = both[cp, t, lo]
                _, tot8, num8 = merge((pk[:8], tot[:8], num[:8]), d)
                o = jnp.concatenate([num8 / tot8, num[8:] / tot[8:]], axis=0)
                a = 256 * cp + 128 * lo + 32 * t
                att[a : a + 32, 128 * t : 128 * t + 128] = jnp.where(lanes, o, 0.0).astype(BF)
        wc = jnp.concatenate([wo[128 * (2 * t + cp) : 128 * (2 * t + cp) + 128, :] for t in range(3)], axis=0)
        y[256 * cp : 256 * cp + 256, :] = dot(att[256 * cp : 256 * cp + 256, :], wc).astype(BF)
    out_ref[...] = dot(back[...], y[...]).astype(BF)
    for c in sent:
        c.wait_send()


def shards(tokens, proj_weight, out_weight):
    hbm = pl.BlockSpec(memory_space=pl.ANY)
    dma = pltpu.SemaphoreType.DMA
    return pl.pallas_call(
        kernel,
        out_shape=jax.ShapeDtypeStruct((512, 768), BF),
        in_specs=[hbm] * 3,
        out_specs=pl.BlockSpec(memory_space=pltpu.VMEM),
        scratch_shapes=[
            pltpu.VMEM((512, 768), BF),
            pltpu.VMEM((512, 512), BF),
            pltpu.VMEM((512, 512), BF),
            pltpu.VMEM((512, 768), BF),
            pltpu.VMEM((768, 2304), BF),
            pltpu.VMEM((768, 768), BF),
            pltpu.VMEM((512, 1152), BF),
            pltpu.VMEM((2, 256, 768), BF),
            pltpu.VMEM((2, 2, 4, 8, 16, 128), BF),
            pltpu.VMEM((8, 16, 128), BF),
            pltpu.VMEM((8, 16, 128), F32),
            pltpu.VMEM((8, 16, 128), F32),
            pltpu.VMEM((512, 384), BF),
            pltpu.VMEM((512, 768), BF),
            dma((3,)),
            dma((24,)), dma((24,)), dma((24,)), dma((24,)),
            dma((8,)), dma((8,)), dma((32,)), dma((32,)),
        ],
        compiler_params=pltpu.CompilerParams(collective_id=0, has_side_effects=True, vmem_limit_bytes=56 << 20),
    )(tokens, proj_weight, out_weight)


def solution(mesh):
    return jax.shard_map(
        shards,
        mesh=mesh,
        in_specs=(P(("wide", "narrow"), None), P("narrow", None), P("narrow", None)),
        out_specs=P(("wide", "narrow"), None),
        check_vma=False,
    )
```

time: 2240 us -> 61.5 us (0.03)
  waiting for transfers between devices: 2110 us -> 0 us
  Pallas kernels: 0 us -> 59.3 us
  blocking collectives: 46 us -> 0 us
  local copies, waits for them, and re-layouts: 37.2 us -> 2.06 us
    all_gather x4 -> x0, waiting for transfers between devices: 2110 us -> none  [the longest x1 1040 us: shards(): lax.all_gather(value_third, ('wide', 'narrow'), axis=0, tiled=True)]
    pallas_call x0 -> x1, Pallas kernels: none -> 59.3 us  [shards(): pl.pallas_call(kernel, out_shape=jax.ShapeDtypeStruct((512, 768), BF), in...]
    all_gather x2 -> x0, blocking collectives: 46 us -> none  [the longest x1 23.3 us: shards(): lax.all_gather(value_second, 'narrow', axis=0, tiled=True)]
  transfers between devices with their start and end apart: 4 -> 0, of which waited for: 4 -> 0; matrix products, arithmetic and copies ran while one was open for 2% -> 0% of each run, Pallas kernels for 0% -> 0%
where the time goes in v1:
time: 61.5 us; the launch traced here: 61.4 us
  Pallas kernels  59.3 us (96%)
  local copies, waits for them, and re-layouts  2.06 us (3%)
    pallas_call x1, Pallas kernels, shards(): pl.pallas_call(kernel, out_shape=jax.ShapeDtypeStruct((512, 768), BF), in...  59.3 us
    unnamed x1, local copies, waits for them, and re-layouts  2.06 us

profile of v1, /device:TPU:1, one launch (start us, length us, event | category | flops | bytes accessed | tf_op | source)
XLA Modules:
  0.0 61.4 jit_solution(3085994859331530219)
XLA Ops:
  0.0 59.3 %shard_map.37 = bf16[512,768]{1,0:T(8,128)(2,1)} custom-call(bf16[512,768]{1,0:T(8,128)(2,1)} %tok_hbm.1, bf16[96,2304]{1,0:T(8,128)(2,1)} %wp_hbm.1, bf16[96,768]{1,0:T(8,128)(2,1)} %wo_hbm.1), custom_call_target="tpu_custom_call" | custom-call | tf_op jit(solution)/shard_map/pallas_call | solution.py:322
  59.3 2.1 %copy.5 = bf16[512,768]{1,0:T(8,128)(2,1)} copy(bf16[512,768]{1,0:T(8,128)(2,1)} %shard_map.37) | data formatting | bytes 1572864

commit v2 on v1

--- a/solution.py
+++ b/solution.py
@@ -48,7 +48,7 @@
 def kernel(
     tok_hbm, wp_hbm, wo_hbm, out_ref,
     tok, perm, back, xp, wp, wo, qkv, kv2, kv3, q3, part_out, part_in, att, y,
-    loc_sem, ws, wr, os_, or_, s2, r2, s3, r3,
+    loc_sem, ws, wr, s2, r2, s3, r3,
 ):
     w, n = lax.axis_index("wide"), lax.axis_index("narrow")
     x, yl, core, z, yh = n % 4, n // 4, w % 2, (w // 2) % 8, w // 16
@@ -57,9 +57,6 @@
     def dev(dx=0, dy=0, dz=0, dc=0):
         y_ = (yy + dy) % 8
         return ((y_ // 2) * 16 + ((z + dz) % 8) * 2 + (core + dc) % 2, (y_ % 2) * 4 + (x + dx) % 4)
-
-    def narrow_dev(k):
-        return (w, (n + k) % 8)
 
     barrier = pltpu.get_barrier_semaphore()
     partners = (
@@ -88,11 +85,13 @@
     pl.semaphore_wait(barrier, len(partners))
 
     class Gather:
-        def __init__(self, src, buf, cuts, ss, rs):
+        def __init__(self, src, buf, base, cuts, ss, rs):
             self.src, self.buf, self.ss, self.rs = src, buf, ss, rs
+            cuts = [base + c for c in cuts]
             q = [pl.ds(a, b - a) for a, b in zip(cuts, cuts[1:])]
             self.q = q
-            self.left, self.right, self.full = pl.ds(0, cuts[2]), pl.ds(cuts[2], cuts[4] - cuts[2]), pl.ds(0, cuts[4])
+            self.left, self.right = pl.ds(cuts[0], cuts[2] - cuts[0]), pl.ds(cuts[2], cuts[4] - cuts[2])
+            self.full = pl.ds(cuts[0], cuts[4] - cuts[0])
             self.sent, self.passed = [], []
             self.k = 0
 
@@ -159,36 +158,43 @@
             for c in self.sent:
                 c.wait_send()
 
-    proj = Gather(wp_hbm, wp, (0, 512, 1152, 1792, 2304), ws, wr)
-    outp = Gather(wo_hbm, wo, (0, 256, 384, 512, 768), os_, or_)
-    proj.phase_a()
+    def group(src, buf, base, k):
+        return Gather(src, buf, base, (0, 128, 384, 512, 768), ws.at[k], wr.at[k])
+
+    gq, gk, gv = (group(wp_hbm, wp, 768 * k, k) for k in range(3))
+    outp = group(wo_hbm, wo, 0, 3)
+    gk.phase_a()
+    gv.phase_a()
 
     perm[...] = jnp.where(iota((512, 512), 1) == tile_of_row(iota((512, 512), 0)), 1.0, 0.0).astype(BF)
-    back[...] = jnp.where(iota((512, 512), 0) == tile_of_row(iota((512, 512), 1)), 1.0, 0.0).astype(BF)
-    proj.phase_b()
+    gk.phase_b()
+    gq.phase_a()
     loc[0].wait()
     xp[...] = dot(perm[...], tok[...]).astype(BF)
-    proj.phase_c()
-    outp.phase_a()
+    gv.phase_b()
+    gk.phase_c()
+    back[...] = jnp.where(iota((512, 512), 0) == tile_of_row(iota((512, 512), 1)), 1.0, 0.0).astype(BF)
+    gq.phase_b()
+    gv.phase_c()
     loc[1].wait()
-    proj.finish()
-
-    for cp in range(2):
-        cols = [768 * m + 128 * (2 * t + cp) for m in range(3) for t in range(3)]
-        wc = jnp.concatenate([wp[:, c : c + 128] for c in cols], axis=1)
-        qkv[256 * cp : 256 * cp + 256, :] = dot(xp[256 * cp : 256 * cp + 256, :], wc).astype(BF)
+
+    def project(m):
+        for cp in range(2):
+            wc = jnp.concatenate([wp[:, c : c + 128] for c in (768 * m + 128 * (2 * t + cp) for t in range(3))], axis=1)
+            r = slice(256 * cp, 256 * cp + 256)
+            qkv[r, 384 * m : 384 * m + 384] = dot(xp[r, :], wc).astype(BF)
 
     low = iota((1, 128), 1) < 64
     row16 = iota((16, 128), 0)
+    zeros8 = jnp.zeros((8, 128), F32)
 
     def second(m, cp, t):
         a = 256 * cp + 32 * t
         c = 384 * m + 128 * t
         return jnp.where(low, qkv[a : a + 32, c : c + 128].astype(F32), qkv[a + 128 : a + 160, c : c + 128].astype(F32))
 
-    zeros8 = jnp.zeros((8, 128), F32)
-    third = [jnp.zeros((16, 128), F32) for _ in range(3)]
-    for m in range(3):
+    def third(m):
+        out = jnp.zeros((16, 128), F32)
         for cp in range(2):
             for t in range(3):
                 v = second(m, cp, t)
@@ -198,13 +204,22 @@
                 e = jnp.concatenate([v[:8], zeros8], axis=0)
                 if i:
                     e = pltpu.roll(e, 2 * i, 0)
-                third[m] = jnp.where((row16 >= 2 * i) & (row16 < 2 * i + 2), e, third[m])
-    q3[z] = third[0].astype(BF)
-    for m in range(2):
-        kv3[m, core, x, yy] = third[m + 1].astype(BF)
+                out = jnp.where((row16 >= 2 * i) & (row16 < 2 * i + 2), e, out)
+        if m > 0:
+            kv3[m - 1, core, x, yy] = out.astype(BF)
+        else:
+            q3[z] = out.astype(BF)
+
+    gk.finish()
+    project(1)
+    third(1)
+    gq.phase_c()
+    gv.finish()
+    project(2)
+    third(2)
 
     sent = []
-    k3 = 0
+    k2 = k3 = 0
 
     def go3(src, dst, to):
         nonlocal k3
@@ -213,13 +228,29 @@
         sent.append(c)
         return c
 
+    def go2(ref, to):
+        nonlocal k2
+        c = send(ref, ref, s2.at[k2], r2.at[k2], to)
+        k2 += 1
+        sent.append(c)
+        return c
+
+    full2, left2, right2 = pl.ds(0, 768), pl.ds(0, 384), pl.ds(384, 384)
+
+    def at2(dx, other, cols=full2):
+        j = ((1 - yl) if other else yl) * 4 + (x + dx) % 4
+        return kv2.at[:, pl.ds(pl.multiple_of(32 * j, 32), 32), cols]
+
     own3 = kv3.at[:, core, x, yy]
-    a3 = [go3(own3, own3, dev(dy=k)) for k in range(1, 8)]
-    sq = [go3(q3.at[z], q3.at[z], dev(dz=k)) for k in range(1, 8)]
-    own2 = kv2.at[:, pl.ds(pl.multiple_of(32 * n, 32), 32)]
-    to2 = [dev(dx=1), dev(dx=3), dev(dx=2), (w, (1 - yl) * 4 + x)] + diag
-    g2 = [send(own2, own2, s2.at[k], r2.at[k], p) for k, p in enumerate(to2)]
-    sent += g2
+    a3 = [go3(own3, own3, dev(dy=k)) for k in (4, 3, 5, 2, 6, 1, 7)]
+    pair = (w, (1 - yl) * 4 + x)
+    u = [go2(at2(0, False), to) for to in (dev(dx=1), dev(dx=3), pair)]
+    outp.phase_a()
+
+    gq.finish()
+    project(0)
+    third(0)
+    sq = [go3(q3.at[z], q3.at[z], dev(dz=k)) for k in (4, 3, 5, 2, 6, 1, 7)]
 
     first = {}
 
@@ -233,15 +264,26 @@
             b = slice(32 * t, 32 * t + 32)
             first[cp, t, lo] = pk[b], tot[b], num[b]
 
-    for t in range(3):
-        level1(0, t)
+    level1(0, 0)
     for c in a3:
         c.wait_recv()
     plane = kv3.at[:, core, x]
-    b3 = [go3(plane, plane, dev(dx=k)) for k in (1, 3, 2)]
-    for t in range(3):
-        level1(1, t)
+    b3 = [go3(plane, plane, dev(dx=k)) for k in (2, 1, 3)]
+    u[0].wait_recv()
+    v1 = go2(at2(3, False, left2), dev(dx=1))
+    u[1].wait_recv()
+    v2 = go2(at2(1, False, right2), dev(dx=3))
+    u[2].wait_recv()
+    g2 = [go2(at2(0, True), dev(dx=1)), go2(at2(0, True), dev(dx=3))]
+    level1(0, 1)
+    level1(0, 2)
     outp.phase_b()
+    level1(1, 0)
+    v1.wait_recv()
+    v2.wait_recv()
+    g2.append(go2(at2(2, False), pair))
+    level1(1, 1)
+    level1(1, 2)
     for c in b3:
         c.wait_recv()
     half = kv3.at[:, core]
@@ -264,7 +306,7 @@
         return jnp.sum(u, axis=1, keepdims=True)
 
     part_out[...] = jnp.where(row < 12, num, jnp.where(row == 12, to_lanes(pk), to_lanes(tot)))
-    sp = [go3(part_out.at[(z + k) % 8], part_in.at[z], dev(dz=k)) for k in range(1, 8)]
+    sp = [go3(part_out.at[(z + k) % 8], part_in.at[z], dev(dz=k)) for k in (4, 3, 5, 2, 6, 1, 7)]
     part_in[z] = part_out[z]
 
     for c in g2:
@@ -340,8 +382,7 @@
             pltpu.VMEM((512, 384), BF),
             pltpu.VMEM((512, 768), BF),
             dma((3,)),
-            dma((24,)), dma((24,)), dma((24,)), dma((24,)),
-            dma((8,)), dma((8,)), dma((32,)), dma((32,)),
+            dma((4, 23)), dma((4, 23)), dma((8,)), dma((8,)), dma((25,)), dma((25,)),
         ],
         compiler_params=pltpu.CompilerParams(collective_id=0, has_side_effects=True, vmem_limit_bytes=56 << 20),
     )(tokens, proj_weight, out_weight)

time: 61.5 us -> 56.5 us (0.919)
  Pallas kernels: 59.3 us -> 54.3 us
    pallas_call x1, Pallas kernels: 59.3 us -> 54.3 us  [shards(): pl.pallas_call(kernel, out_shape=jax.ShapeDtypeStruct((512, 768), BF), in...]
where the time goes in v2:
time: 56.5 us; the launch traced here: 56.3 us
  Pallas kernels  54.3 us (96%)
  local copies, waits for them, and re-layouts  2.06 us (4%)
    pallas_call x1, Pallas kernels, shards(): pl.pallas_call(kernel, out_shape=jax.ShapeDtypeStruct((512, 768), BF), in...  54.3 us
    unnamed x1, local copies, waits for them, and re-layouts  2.06 us

profile of v2, /device:TPU:1, one launch (start us, length us, event | category | flops | bytes accessed | tf_op | source)
XLA Modules:
  0.0 56.3 jit_solution(11741080880957929152)
XLA Ops:
  0.0 54.3 %shard_map.37 = bf16[512,768]{1,0:T(8,128)(2,1)} custom-call(bf16[512,768]{1,0:T(8,128)(2,1)} %tok_hbm.1, bf16[96,2304]{1,0:T(8,128)(2,1)} %wp_hbm.1, bf16[96,768]{1,0:T(8,128)(2,1)} %wo_hbm.1), custom_call_target="tpu_custom_call" | custom-call | tf_op jit(solution)/shard_map/pallas_call | solution.py:364
  54.3 2.1 %copy.5 = bf16[512,768]{1,0:T(8,128)(2,1)} copy(bf16[512,768]{1,0:T(8,128)(2,1)} %shard_map.37) | data formatting | bytes 1572864

commit v3 on v2

v3 whole, which is shorter than its diff:
```python
import jax
import jax.numpy as jnp
from jax import lax
from jax.experimental import pallas as pl
from jax.experimental.pallas import tpu as pltpu
from jax.sharding import PartitionSpec as P

MESH = pl.DeviceIdType.MESH
BF = jnp.bfloat16
F32 = jnp.float32
SCALE = 0.125
LOW = -1e30


def iota(shape, dim):
    return lax.broadcasted_iota(jnp.int32, shape, dim)


def tile_of_row(r, core):
    j = r % 32
    s = jnp.where(j == 1, 16, jnp.where((j >= 2) & (j <= 16), j - 1, j))
    return 16 * s + 4 * ((r // 32) % 4) + 2 * ((r // 256 + core) % 2) + (r // 128) % 2


def dot(a, b):
    return jnp.dot(a, b, preferred_element_type=F32)


def dot_t(a, b):
    return lax.dot_general(a, b, (((1,), (1,)), ((), ())), preferred_element_type=F32)


def soft(q, k, v, mask=None):
    s = dot_t(q, k) * SCALE
    if mask is not None:
        s = jnp.where(mask, s, LOW)
    peak = jnp.max(s, axis=-1, keepdims=True)
    w = jnp.exp(s - peak)
    return peak, jnp.sum(w, axis=-1, keepdims=True), dot(w.astype(BF), v)


def merge(a, b):
    top = jnp.maximum(a[0], b[0])
    ea, eb = jnp.exp(a[0] - top), jnp.exp(b[0] - top)
    return top, a[1] * ea + b[1] * eb, a[2] * ea + b[2] * eb


def kernel(
    tok_hbm, wp_hbm, wo_hbm, out_ref,
    tok, perm, back, xs, xo, wp, wo, qkv, kv2, kv3, q3, part_out, part_in, att, got, y,
    loc_sem, ws, wr, os_, or_, s2, r2, s3, r3, sc, rc,
):
    w, n = lax.axis_index("wide"), lax.axis_index("narrow")
    x, yl, core, z, yh = n % 4, n // 4, w % 2, (w // 2) % 8, w // 16
    yy = 2 * yh + yl

    def dev(dx=0, dy=0, dz=0, dc=0):
        y_ = (yy + dy) % 8
        return ((y_ // 2) * 16 + ((z + dz) % 8) * 2 + (core + dc) % 2, (y_ % 2) * 4 + (x + dx) % 4)

    barrier = pltpu.get_barrier_semaphore()
    partners = (
        [dev(dx=k) for k in (1, 2, 3)] + [dev(dy=k) for k in range(1, 8)] + [dev(dz=k) for k in range(1, 8)] + [dev(dc=1)]
    )
    for p in partners:
        pl.semaphore_signal(barrier, inc=1, device_id=p, device_id_type=MESH)

    def send(src, dst, ss, rs, to):
        c = pltpu.make_async_remote_copy(
            src_ref=src, dst_ref=dst, send_sem=ss, recv_sem=rs, device_id=to, device_id_type=MESH
        )
        c.start()
        return c

    mine = pl.ds(pl.multiple_of(96 * n, 32), 96)
    loc = [
        pltpu.make_async_copy(tok_hbm, tok, loc_sem.at[0]),
        pltpu.make_async_copy(wo_hbm, wo.at[mine], loc_sem.at[1]),
    ]
    for m in range(3):
        for t in range(3):
            src = wp_hbm.at[:, pl.ds(pl.multiple_of(768 * m + 256 * t + 128 * core, 128), 128)]
            dst = wp.at[mine, pl.ds(384 * m + 128 * t, 128)]
            loc.append(pltpu.make_async_copy(src, dst, loc_sem.at[2 + 3 * m + t]))
    for c in loc[2:] + loc[:2]:
        c.start()
    perm[...] = jnp.where(iota((512, 512), 1) == tile_of_row(iota((512, 1), 0), core), 1.0, 0.0).astype(BF)
    back[...] = jnp.where(iota((512, 512), 0) == tile_of_row(iota((1, 512), 1), core), 1.0, 0.0).astype(BF)
    for c in loc[2:]:
        c.wait()
    pl.semaphore_wait(barrier, len(partners))

    class Rows:
        def __init__(self, m, ss, rs):
            self.cols, self.ss, self.rs = pl.ds(384 * m, 384), ss, rs
            self.sent = []

        def go(self, dx, other, first, count, to):
            j = ((1 - yl) if other else yl) * 4 + (x + dx) % 4
            ref = wp.at[pl.ds(pl.multiple_of(96 * j + first, 16), count), self.cols]
            k = len(self.sent)
            c = send(ref, ref, self.ss.at[k], self.rs.at[k], to)
            self.sent.append(c)
            return c

        def phase_a(self):
            self.a = [self.go(0, False, 0, 96, dev(dx=1)), self.go(0, False, 0, 96, dev(dx=3))]
            self.a += [self.go(0, False, 0, 48, dev(dy=1)), self.go(0, False, 48, 48, dev(dy=7))]

        def phase_b(self):
            self.a[0].wait_recv()
            b1, b3 = self.go(3, False, 0, 48, dev(dx=1)), self.go(3, False, 0, 96, dev(dy=1))
            self.a[1].wait_recv()
            b2, b4 = self.go(1, False, 48, 48, dev(dx=3)), self.go(1, False, 0, 96, dev(dy=7))
            self.b = [b1, b2, b3, b4]

        def phase_c(self):
            b1, b2, b3, b4 = self.b
            b1.wait_recv()
            c3 = self.go(2, False, 0, 16, dev(dy=1))
            b2.wait_recv()
            c4 = self.go(2, False, 64, 32, dev(dy=7))
            b3.wait_recv()
            c1 = self.go(3, True, 16, 32, dev(dx=1))
            b4.wait_recv()
            c2 = self.go(1, True, 48, 16, dev(dx=3))
            self.c = [c1, c2, c3, c4]

        def finish(self):
            for c in self.a[2:] + self.c:
                c.wait_recv()

    class Twin:
        def __init__(self):
            self.sent, self.passed = [], []
            self.left, self.right, self.full = pl.ds(0, 384), pl.ds(384, 384), pl.ds(0, 768)

        def at(self, dx, other, cols):
            j = ((1 - yl) if other else yl) * 4 + (x + dx) % 4
            return wo.at[pl.ds(pl.multiple_of(96 * j + 48 * core, 16), 48), cols]

        def go(self, ref, to):
            k = len(self.sent)
            c = send(ref, ref, os_.at[k], or_.at[k], to)
            self.sent.append(c)
            return c

        def twin(self, *refs):
            for ref in refs:
                self.passed.append(self.go(ref, dev(dc=1)))

        def phase_ax(self):
            self.a = [self.go(self.at(0, False, self.full), dev(dx=k)) for k in (1, 3, 2)]

        def phase_ay(self):
            self.a.append(self.go(self.at(0, False, self.left), dev(dy=1)))
            self.a.append(self.go(self.at(0, False, self.right), dev(dy=7)))

        def phase_b(self):
            a = self.a
            a[0].wait_recv()
            self.b = [self.go(self.at(3, False, self.full), dev(dy=1))]
            a[1].wait_recv()
            self.b.append(self.go(self.at(1, False, self.full), dev(dy=7)))
            a[2].wait_recv()
            self.b.append(self.go(self.at(2, False, self.left), dev(dy=1)))
            self.b.append(self.go(self.at(2, False, self.right), dev(dy=7)))
            self.twin(*[self.at(k, False, self.full) for k in (1, 2, 3)])
            a[3].wait_recv()
            a[4].wait_recv()
            self.twin(self.at(0, True, self.full))

        def phase_c(self):
            for c in self.b:
                c.wait_recv()
            self.twin(*[self.at(k, True, self.full) for k in (1, 2, 3)])

        def finish(self):
            for c in self.passed:
                c.wait_recv()

    gq, gk, gv = (Rows(m, ws.at[m], wr.at[m]) for m in range(3))
    outp = Twin()
    weights = (gk, gv, gq)
    for g in weights:
        g.phase_a()
    loc[0].wait()
    xo[...] = dot(perm[256:, :], tok[...]).astype(BF)
    tokens_sent = send(xo, xs.at[pl.ds(256, 256)], sc.at[0], rc.at[0], dev(dc=1))
    gk.phase_b()
    xs[:256, :] = dot(perm[:256, :], tok[...]).astype(BF)
    gv.phase_b()
    gq.phase_b()
    for g in weights:
        g.phase_c()

    def project(m):
        qkv[:, 384 * m : 384 * m + 384] = dot(xs[...], wp[:, 384 * m : 384 * m + 384]).astype(BF)

    low = iota((1, 128), 1) < 64
    row16 = iota((16, 128), 0)
    zeros8 = jnp.zeros((8, 128), F32)
    mine2 = pl.ds(pl.multiple_of(32 * n, 32), 32)

    def second(m, e, t):
        a = 256 * e + 32 * t
        c = 384 * m + 128 * t
        return jnp.where(low, qkv[a : a + 32, c : c + 128].astype(F32), qkv[a + 128 : a + 160, c : c + 128].astype(F32))

    def third(m):
        out = jnp.zeros((16, 128), F32)
        for e in range(2):
            for t in range(3):
                v = second(m, e, t)
                i = 4 * t + 2 * e
                if m > 0:
                    kv2[m - 1, e, mine2, 128 * t : 128 * t + 128] = v.astype(BF)
                u = jnp.concatenate([v[:8], zeros8], axis=0)
                if i:
                    u = pltpu.roll(u, i, 0)
                out = jnp.where((row16 >= i) & (row16 < i + 2), u, out)
        if m > 0:
            kv3[m - 1, x, yy] = out.astype(BF)
        else:
            q3[z] = out.astype(BF)

    tokens_sent.wait_recv()
    gk.finish()
    project(1)
    third(1)
    gv.finish()
    project(2)
    third(2)

    sent = [tokens_sent]
    k2 = k3 = 0

    def go3(src, dst, to):
        nonlocal k3
        c = send(src, dst, s3.at[k3], r3.at[k3], to)
        k3 += 1
        sent.append(c)
        return c

    def go2(ref, to):
        nonlocal k2
        c = send(ref, ref, s2.at[k2], r2.at[k2], to)
        k2 += 1
        sent.append(c)
        return c

    def at2(dx, other, e=None):
        j = ((1 - yl) if other else yl) * 4 + (x + dx) % 4
        return kv2.at[:, pl.ds(0, 2) if e is None else pl.ds(e, 1), pl.ds(pl.multiple_of(32 * j, 32), 32)]

    own3 = kv3.at[:, x, yy]
    a3 = [go3(own3, own3, dev(dy=k)) for k in (4, 3, 5, 2, 6, 1, 7)]
    pair = (w, (1 - yl) * 4 + x)
    u = [go2(at2(0, False), to) for to in (dev(dx=1), dev(dx=3))]
    loc[1].wait()
    outp.phase_ax()

    gq.finish()
    project(0)
    third(0)
    sq = [go3(q3.at[z], q3.at[z], dev(dz=k)) for k in (4, 3, 5, 2, 6, 1, 7)]

    first = {}

    def level1(e, t):
        o = []
        for lo in range(2):
            r = slice(256 * e + 128 * lo, 256 * e + 128 * lo + 128)
            q = jnp.where(low if lo == 0 else ~low, qkv[r, 128 * t : 128 * t + 128].astype(F32), 0.0).astype(BF)
            pk, tot, num = soft(q, qkv[r, 384 + 128 * t : 512 + 128 * t], qkv[r, 768 + 128 * t : 896 + 128 * t])
            o.append(num / tot)
            b = slice(32 * t, 32 * t + 32)
            first[e, t, lo] = pk[b], tot[b], num[b]
        att[e, :, 128 * t : 128 * t + 128] = jnp.where(low, o[0], o[1]).astype(BF)

    level1(0, 0)
    for c in a3:
        c.wait_recv()
    plane = kv3.at[:, x]
    b3 = [go3(plane, plane, dev(dx=k)) for k in (2, 1, 3)]
    u.append(go2(at2(0, False), pair))
    outp.phase_ay()
    u[0].wait_recv()
    v1 = go2(at2(3, False, 0), dev(dx=1))
    u[1].wait_recv()
    v2 = go2(at2(1, False, 1), dev(dx=3))
    level1(0, 1)
    level1(0, 2)
    u[2].wait_recv()
    g2 = [go2(at2(0, True), dev(dx=1)), go2(at2(0, True), dev(dx=3))]
    for c in b3 + sq:
        c.wait_recv()

    qa = q3[...].reshape(128, 128).astype(F32)
    qs = jnp.concatenate([jnp.where(low, qa, 0.0), jnp.where(low, 0.0, qa)], axis=0).astype(BF)
    same = (iota((256, 512), 0) % 16) // 4 == (iota((256, 512), 1) % 16) // 4
    pk, tot, num = soft(qs, kv3[0].reshape(512, 128), kv3[1].reshape(512, 128), same)
    num = jnp.where(low, num[:128], num[128:]).reshape(8, 16, 128)
    row, lane = iota((8, 16, 128), 1), iota((8, 16, 128), 2)

    def to_lanes(v):
        a, b = v[:128].reshape(8, 16, 1), v[128:].reshape(8, 16, 1)
        u = jnp.where(lane == row, a, jnp.where(lane == row + 64, b, 0.0))
        return jnp.sum(u, axis=1, keepdims=True)

    part_out[...] = jnp.where(row < 12, num, jnp.where(row == 12, to_lanes(pk), to_lanes(tot)))
    sp = [go3(part_out.at[(z + k) % 8], part_in.at[z], dev(dz=k)) for k in (4, 3, 5, 2, 6, 1, 7)]
    part_in[z] = part_out[z]
    v1.wait_recv()
    v2.wait_recv()
    g2.append(go2(at2(2, False), pair))
    outp.phase_b()
    for t in range(3):
        level1(1, t)
    outp.phase_c()

    for c in g2:
        c.wait_recv()
    both = {}
    for e in range(2):
        for t in range(3):
            v = second(0, e, t)
            q = jnp.concatenate([jnp.where(low, v, 0.0), jnp.where(low, 0.0, v)], axis=0).astype(BF)
            pk, tot, num = soft(q, kv2[0, e, :, 128 * t : 128 * t + 128], kv2[1, e, :, 128 * t : 128 * t + 128])
            for lo in range(2):
                b = slice(32 * lo, 32 * lo + 32)
                both[e, t, lo] = merge(first[e, t, lo], (pk[b], tot[b], num[b]))

    outp.finish()
    for c in sp:
        c.wait_recv()
    p = part_in[...]

    def from_lanes(v):
        a = jnp.sum(jnp.where(lane == row, v, 0.0), axis=-1, keepdims=True)
        b = jnp.sum(jnp.where(lane == row + 64, v, 0.0), axis=-1, keepdims=True)
        return jnp.where(lane < 64, a, b)

    pk, tot = from_lanes(p[:, 12:13]), from_lanes(p[:, 13:14])
    top = jnp.max(pk, axis=0)
    f = jnp.exp(pk - top[None])
    dist = (top, jnp.sum(tot * f, axis=0), jnp.sum(p * f, axis=0))

    use = iota((8, 128), 0) < 2

    def complete(e):
        for t in range(3):
            i = 4 * t + 2 * e
            d = [pltpu.roll(v, 16 - i, 0)[:8] if i else v[:8] for v in dist]
            d = (jnp.where(use, d[0], LOW), jnp.where(use, d[1], 0.0), jnp.where(use, d[2], 0.0))
            o = []
            for lo in range(2):
                pk, tot, num = both[e, t, lo]
                _, tot8, num8 = merge((pk[:8], tot[:8], num[:8]), d)
                o.append(jnp.concatenate([num8 / tot8, num[8:] / tot[8:]], axis=0))
            att[e, 32 * t : 32 * t + 32, 128 * t : 128 * t + 128] = jnp.where(low, o[0], o[1]).astype(BF)

    low384 = iota((1, 384), 1) % 128 < 64

    def output(e, packed):
        v = packed.astype(F32)
        rows = jnp.concatenate([jnp.where(low384, v, 0.0), jnp.where(low384, 0.0, v)], axis=0).astype(BF)
        at = [256 * t + 128 * ((core + e) % 2) for t in range(3)]
        wc = jnp.concatenate([wo[pl.ds(pl.multiple_of(a, 128), 128), :] for a in at], axis=0)
        y[256 * e : 256 * e + 256, :] = dot(rows, wc).astype(BF)

    complete(1)
    swap = send(att.at[1], got, sc.at[1], rc.at[1], dev(dc=1))
    sent.append(swap)
    complete(0)
    output(0, att[0])
    swap.wait_recv()
    output(1, got[...])
    out_ref[...] = dot(back[...], y[...]).astype(BF)
    for g in weights + (outp,):
        sent += g.sent
    for c in sent:
        c.wait_send()


def shards(tokens, proj_weight, out_weight):
    hbm = pl.BlockSpec(memory_space=pl.ANY)
    dma = pltpu.SemaphoreType.DMA
    return pl.pallas_call(
        kernel,
        out_shape=jax.ShapeDtypeStruct((512, 768), BF),
        in_specs=[hbm] * 3,
        out_specs=pl.BlockSpec(memory_space=pltpu.VMEM),
        scratch_shapes=[
            pltpu.VMEM((512, 768), BF),
            pltpu.VMEM((512, 512), BF),
            pltpu.VMEM((512, 512), BF),
            pltpu.VMEM((512, 768), BF),
            pltpu.VMEM((256, 768), BF),
            pltpu.VMEM((768, 1152), BF),
            pltpu.VMEM((768, 768), BF),
            pltpu.VMEM((512, 1152), BF),
            pltpu.VMEM((2, 2, 256, 384), BF),
            pltpu.VMEM((2, 4, 8, 16, 128), BF),
            pltpu.VMEM((8, 16, 128), BF),
            pltpu.VMEM((8, 16, 128), F32),
            pltpu.VMEM((8, 16, 128), F32),
            pltpu.VMEM((2, 128, 384), BF),
            pltpu.VMEM((128, 384), BF),
            pltpu.VMEM((512, 768), BF),
            dma((11,)),
            dma((3, 12)), dma((3, 12)), dma((16,)), dma((16,)),
            dma((8,)), dma((8,)), dma((24,)), dma((24,)), dma((2,)), dma((2,)),
        ],
        compiler_params=pltpu.CompilerParams(collective_id=0, has_side_effects=True, vmem_limit_bytes=56 << 20),
    )(tokens, proj_weight, out_weight)


def solution(mesh):
    return jax.shard_map(
        shards,
        mesh=mesh,
        in_specs=(P(("wide", "narrow"), None), P("narrow", None), P("narrow", None)),
        out_specs=P(("wide", "narrow"), None),
        check_vma=False,
    )
```

time: 56.5 us -> 52.2 us (0.924)
  Pallas kernels: 54.3 us -> 50 us
    pallas_call x1, Pallas kernels: 54.3 us -> 50 us  [shards(): pl.pallas_call(kernel, out_shape=jax.ShapeDtypeStruct((512, 768), BF), in...]
where the time goes in v3:
time: 52.2 us; the launch traced here: 52 us
  Pallas kernels  50 us (96%)
  local copies, waits for them, and re-layouts  2.06 us (4%)
    pallas_call x1, Pallas kernels, shards(): pl.pallas_call(kernel, out_shape=jax.ShapeDtypeStruct((512, 768), BF), in...  50 us
    unnamed x1, local copies, waits for them, and re-layouts  2.06 us

profile of v3, /device:TPU:1, one launch (start us, length us, event | category | flops | bytes accessed | tf_op | source)
XLA Modules:
  0.0 52.0 jit_solution(11240641202168621296)
XLA Ops:
  0.0 50.0 %shard_map.37 = bf16[512,768]{1,0:T(8,128)(2,1)} custom-call(bf16[512,768]{1,0:T(8,128)(2,1)} %tok_hbm.1, bf16[96,2304]{1,0:T(8,128)(2,1)} %wp_hbm.1, bf16[96,768]{1,0:T(8,128)(2,1)} %wo_hbm.1), custom_call_target="tpu_custom_call" | custom-call | tf_op jit(solution)/shard_map/pallas_call | solution.py:389
  50.0 2.1 %copy.5 = bf16[512,768]{1,0:T(8,128)(2,1)} copy(bf16[512,768]{1,0:T(8,128)(2,1)} %shard_map.37) | data formatting | bytes 1572864

commit v4 on v3

--- a/solution.py
+++ b/solution.py
@@ -46,8 +46,8 @@
 
 
 def kernel(
-    tok_hbm, wp_hbm, wo_hbm, out_ref,
-    tok, perm, back, xs, xo, wp, wo, qkv, kv2, kv3, q3, part_out, part_in, att, got, y,
+    tok_hbm, wp_hbm, wo_hbm, y,
+    tok, perm, xs, xo, wp, wo, qkv, kv2, kv3, q3, part_out, part_in, att, got,
     loc_sem, ws, wr, os_, or_, s2, r2, s3, r3, sc, rc,
 ):
     w, n = lax.axis_index("wide"), lax.axis_index("narrow")
@@ -80,54 +80,42 @@
     for m in range(3):
         for t in range(3):
             src = wp_hbm.at[:, pl.ds(pl.multiple_of(768 * m + 256 * t + 128 * core, 128), 128)]
-            dst = wp.at[mine, pl.ds(384 * m + 128 * t, 128)]
+            dst = wp.at[m, mine, pl.ds(128 * t, 128)]
             loc.append(pltpu.make_async_copy(src, dst, loc_sem.at[2 + 3 * m + t]))
     for c in loc[2:] + loc[:2]:
         c.start()
     perm[...] = jnp.where(iota((512, 512), 1) == tile_of_row(iota((512, 1), 0), core), 1.0, 0.0).astype(BF)
-    back[...] = jnp.where(iota((512, 512), 0) == tile_of_row(iota((1, 512), 1), core), 1.0, 0.0).astype(BF)
     for c in loc[2:]:
         c.wait()
     pl.semaphore_wait(barrier, len(partners))
 
     class Rows:
         def __init__(self, m, ss, rs):
-            self.cols, self.ss, self.rs = pl.ds(384 * m, 384), ss, rs
+            self.buf, self.ss, self.rs = wp.at[m], ss, rs
             self.sent = []
 
         def go(self, dx, other, first, count, to):
             j = ((1 - yl) if other else yl) * 4 + (x + dx) % 4
-            ref = wp.at[pl.ds(pl.multiple_of(96 * j + first, 16), count), self.cols]
+            ref = self.buf.at[pl.ds(pl.multiple_of(96 * j + first, 16), count)]
             k = len(self.sent)
             c = send(ref, ref, self.ss.at[k], self.rs.at[k], to)
             self.sent.append(c)
             return c
 
         def phase_a(self):
-            self.a = [self.go(0, False, 0, 96, dev(dx=1)), self.go(0, False, 0, 96, dev(dx=3))]
+            self.a = [self.go(0, False, 0, 96, dev(dx=k)) for k in (1, 3, 2)]
             self.a += [self.go(0, False, 0, 48, dev(dy=1)), self.go(0, False, 48, 48, dev(dy=7))]
 
         def phase_b(self):
             self.a[0].wait_recv()
-            b1, b3 = self.go(3, False, 0, 48, dev(dx=1)), self.go(3, False, 0, 96, dev(dy=1))
+            self.b = [self.go(3, False, 0, 96, dev(dy=1))]
             self.a[1].wait_recv()
-            b2, b4 = self.go(1, False, 48, 48, dev(dx=3)), self.go(1, False, 0, 96, dev(dy=7))
-            self.b = [b1, b2, b3, b4]
-
-        def phase_c(self):
-            b1, b2, b3, b4 = self.b
-            b1.wait_recv()
-            c3 = self.go(2, False, 0, 16, dev(dy=1))
-            b2.wait_recv()
-            c4 = self.go(2, False, 64, 32, dev(dy=7))
-            b3.wait_recv()
-            c1 = self.go(3, True, 16, 32, dev(dx=1))
-            b4.wait_recv()
-            c2 = self.go(1, True, 48, 16, dev(dx=3))
-            self.c = [c1, c2, c3, c4]
+            self.b.append(self.go(1, False, 0, 96, dev(dy=7)))
+            self.a[2].wait_recv()
+            self.b += [self.go(2, False, 0, 48, dev(dy=1)), self.go(2, False, 48, 48, dev(dy=7))]
 
         def finish(self):
-            for c in self.a[2:] + self.c:
+            for c in self.a[3:] + self.b:
                 c.wait_recv()
 
     class Twin:
@@ -191,11 +179,12 @@
     xs[:256, :] = dot(perm[:256, :], tok[...]).astype(BF)
     gv.phase_b()
     gq.phase_b()
-    for g in weights:
-        g.phase_c()
+    loc[1].wait()
+    outp.phase_ax()
+    outp.phase_ay()
 
     def project(m):
-        qkv[:, 384 * m : 384 * m + 384] = dot(xs[...], wp[:, 384 * m : 384 * m + 384]).astype(BF)
+        qkv[:, 384 * m : 384 * m + 384] = dot(xs[...], wp[m]).astype(BF)
 
     low = iota((1, 128), 1) < 64
     row16 = iota((16, 128), 0)
@@ -257,13 +246,11 @@
     a3 = [go3(own3, own3, dev(dy=k)) for k in (4, 3, 5, 2, 6, 1, 7)]
     pair = (w, (1 - yl) * 4 + x)
     u = [go2(at2(0, False), to) for to in (dev(dx=1), dev(dx=3))]
-    loc[1].wait()
-    outp.phase_ax()
-
     gq.finish()
     project(0)
     third(0)
     sq = [go3(q3.at[z], q3.at[z], dev(dz=k)) for k in (4, 3, 5, 2, 6, 1, 7)]
+    u.append(go2(at2(0, False), pair))
 
     first = {}
 
@@ -278,19 +265,17 @@
             first[e, t, lo] = pk[b], tot[b], num[b]
         att[e, :, 128 * t : 128 * t + 128] = jnp.where(low, o[0], o[1]).astype(BF)
 
-    level1(0, 0)
     for c in a3:
         c.wait_recv()
     plane = kv3.at[:, x]
     b3 = [go3(plane, plane, dev(dx=k)) for k in (2, 1, 3)]
-    u.append(go2(at2(0, False), pair))
-    outp.phase_ay()
     u[0].wait_recv()
     v1 = go2(at2(3, False, 0), dev(dx=1))
     u[1].wait_recv()
     v2 = go2(at2(1, False, 1), dev(dx=3))
+    outp.phase_b()
+    level1(0, 0)
     level1(0, 1)
-    level1(0, 2)
     u[2].wait_recv()
     g2 = [go2(at2(0, True), dev(dx=1)), go2(at2(0, True), dev(dx=3))]
     for c in b3 + sq:
@@ -314,7 +299,7 @@
     v1.wait_recv()
     v2.wait_recv()
     g2.append(go2(at2(2, False), pair))
-    outp.phase_b()
+    level1(0, 2)
     for t in range(3):
         level1(1, t)
     outp.phase_c()
@@ -376,17 +361,23 @@
     output(0, att[0])
     swap.wait_recv()
     output(1, got[...])
-    out_ref[...] = dot(back[...], y[...]).astype(BF)
     for g in weights + (outp,):
         sent += g.sent
     for c in sent:
         c.wait_send()
 
 
+def in_order(y, out_ref):
+    core = lax.axis_index("wide") % 2
+    p = iota((256, 512), 0) + 256 * pl.program_id(0)
+    back = jnp.where(p == tile_of_row(iota((1, 512), 1), core), 1.0, 0.0).astype(BF)
+    out_ref[...] = dot(back, y[...]).astype(BF)
+
+
 def shards(tokens, proj_weight, out_weight):
     hbm = pl.BlockSpec(memory_space=pl.ANY)
     dma = pltpu.SemaphoreType.DMA
-    return pl.pallas_call(
+    rows = pl.pallas_call(
         kernel,
         out_shape=jax.ShapeDtypeStruct((512, 768), BF),
         in_specs=[hbm] * 3,
@@ -394,10 +385,9 @@
         scratch_shapes=[
             pltpu.VMEM((512, 768), BF),
             pltpu.VMEM((512, 512), BF),
-            pltpu.VMEM((512, 512), BF),
             pltpu.VMEM((512, 768), BF),
             pltpu.VMEM((256, 768), BF),
-            pltpu.VMEM((768, 1152), BF),
+            pltpu.VMEM((3, 768, 384), BF),
             pltpu.VMEM((768, 768), BF),
             pltpu.VMEM((512, 1152), BF),
             pltpu.VMEM((2, 2, 256, 384), BF),
@@ -407,13 +397,20 @@
             pltpu.VMEM((8, 16, 128), F32),
             pltpu.VMEM((2, 128, 384), BF),
             pltpu.VMEM((128, 384), BF),
-            pltpu.VMEM((512, 768), BF),
             dma((11,)),
             dma((3, 12)), dma((3, 12)), dma((16,)), dma((16,)),
             dma((8,)), dma((8,)), dma((24,)), dma((24,)), dma((2,)), dma((2,)),
         ],
         compiler_params=pltpu.CompilerParams(collective_id=0, has_side_effects=True, vmem_limit_bytes=56 << 20),
     )(tokens, proj_weight, out_weight)
+    return pl.pallas_call(
+        in_order,
+        out_shape=jax.ShapeDtypeStruct((512, 768), BF),
+        grid=(2,),
+        in_specs=[pl.BlockSpec((512, 768), lambda i: (0, 0))],
+        out_specs=pl.BlockSpec((256, 768), lambda i: (i, 0)),
+        compiler_params=pltpu.CompilerParams(vmem_limit_bytes=16 << 20),
+    )(rows)
 
 
 def solution(mesh):

time: 52.2 us -> 50.6 us (0.969)
  local copies, waits for them, and re-layouts: 2.06 us -> 1.13 us
  Pallas kernels: 50 us -> 49.2 us
    pallas_call x1, Pallas kernels: 50 us -> 47.7 us  [shards(): pl.pallas_call(kernel, out_shape=jax.ShapeDtypeStruct((512, 768), BF), in...]
    pallas_call x0 -> x1, Pallas kernels: none -> 1.52 us  [shards(): pl.pallas_call(in_order, out_shape=jax.ShapeDtypeStruct((512, 768), BF),...]
    unnamed x1 -> x2, local copies, waits for them, and re-layouts: 2.06 us -> 1.13 us
where the time goes in v4:
time: 50.6 us; the launch traced here: 50.4 us
  Pallas kernels  49.2 us (97%)
  local copies, waits for them, and re-layouts  1.13 us (2%)
    pallas_call x1, Pallas kernels, shards(): pl.pallas_call(kernel, out_shape=jax.ShapeDtypeStruct((512, 768), BF), in...  47.7 us
    pallas_call x1, Pallas kernels, shards(): pl.pallas_call(in_order, out_shape=jax.ShapeDtypeStruct((512, 768), BF),...  1.52 us
    unnamed x2, local copies, waits for them, and re-layouts  1.13 us

profile of v4, /device:TPU:1, one launch (start us, length us, event | category | flops | bytes accessed | tf_op | source)
XLA Modules:
  0.0 50.4 jit_solution(7598402811878970117)
XLA Ops:
  0.0 47.7 %shard_map.37.y = bf16[512,768]{1,0:T(8,128)(2,1)} custom-call(bf16[512,768]{1,0:T(8,128)(2,1)} %tok_hbm.1, bf16[96,2304]{1,0:T(8,128)(2,1)} %wp_hbm.1, bf16[96,768]{1,0:T(8,128)(2,1)} %wo_hbm.1), custom_call_target="tpu_custom_call" | custom-call | tf_op jit(solution)/shard_map/pallas_call | solution.py:380
  47.7 0.0 copy-start
  47.7 1.1 %copy-done = bf16[512,768]{1,0:T(8,128)(2,1)S(1)} copy-done((bf16[512,768]{1,0:T(8,128)(2,1)S(1)}, bf16[512,768]{1,0:T(8,128)(2,1)}, u32[]{:S(2)}) %copy-start) | copy-done | bytes 786456
  48.9 1.5 %shard_map.38 = bf16[512,768]{1,0:T(8,128)(2,1)} custom-call(bf16[512,768]{1,0:T(8,128)(2,1)S(1)} %copy-done), custom_call_target="tpu_custom_call" | custom-call | tf_op jit(solution)/shard_map/pallas_call | solution.py:406
Async XLA Ops:
  47.7 1.1 %copy-start = (bf16[512,768]{1,0:T(8,128)(2,1)S(1)}, bf16[512,768]{1,0:T(8,128)(2,1)}, u32[]{:S(2)}) copy-start(bf16[512,768]{1,0:T(8,128)(2,1)} %shard_map.37.y) | copy-start | bytes 2359300

commit v5 on v4

--- a/solution.py
+++ b/solution.py
@@ -317,6 +317,11 @@
                 both[e, t, lo] = merge(first[e, t, lo], (pk[b], tot[b], num[b]))
 
     outp.finish()
+    for g in weights + (outp,):
+        sent += g.sent
+    for c in sent:
+        if not any(c is d for d in sp):
+            c.wait_send()
     for c in sp:
         c.wait_recv()
     p = part_in[...]
@@ -356,14 +361,11 @@
 
     complete(1)
     swap = send(att.at[1], got, sc.at[1], rc.at[1], dev(dc=1))
-    sent.append(swap)
     complete(0)
     output(0, att[0])
     swap.wait_recv()
     output(1, got[...])
-    for g in weights + (outp,):
-        sent += g.sent
-    for c in sent:
+    for c in sp + [swap]:
         c.wait_send()
 
 
@@ -379,7 +381,7 @@
     dma = pltpu.SemaphoreType.DMA
     rows = pl.pallas_call(
         kernel,
-        out_shape=jax.ShapeDtypeStruct((512, 768), BF),
+        out_shape=pltpu.VMEM((512, 768), BF),
         in_specs=[hbm] * 3,
         out_specs=pl.BlockSpec(memory_space=pltpu.VMEM),
         scratch_shapes=[
@@ -407,7 +409,7 @@
         in_order,
         out_shape=jax.ShapeDtypeStruct((512, 768), BF),
         grid=(2,),
-        in_specs=[pl.BlockSpec((512, 768), lambda i: (0, 0))],
+        in_specs=[pl.BlockSpec(memory_space=pltpu.VMEM)],
         out_specs=pl.BlockSpec((256, 768), lambda i: (i, 0)),
         compiler_params=pltpu.CompilerParams(vmem_limit_bytes=16 << 20),
     )(rows)

time: 50.6 us -> 48.5 us (0.958)
  local copies, waits for them, and re-layouts: 1.13 us -> 0 us
  Pallas kernels: 49.2 us -> 48.3 us
    unnamed x2 -> x0, local copies, waits for them, and re-layouts: 1.13 us -> none
    pallas_call x1, Pallas kernels: 47.7 us -> 46.8 us  [shards(): pl.pallas_call(kernel, out_shape=pltpu.VMEM((512, 768), BF), in_specs=[hb...]
where the time goes in v5:
time: 48.5 us; the launch traced here: 48.3 us
  Pallas kernels  48.3 us (100%)
    pallas_call x1, Pallas kernels, shards(): pl.pallas_call(kernel, out_shape=pltpu.VMEM((512, 768), BF), in_specs=[hb...  46.8 us
    pallas_call x1, Pallas kernels, shards(): pl.pallas_call(in_order, out_shape=jax.ShapeDtypeStruct((512, 768), BF),...  1.54 us

profile of v5, /device:TPU:1, one launch (start us, length us, event | category | flops | bytes accessed | tf_op | source)
XLA Modules:
  0.0 48.3 jit_solution(17014435571762609807)
XLA Ops:
  0.0 46.8 %shard_map.37.y = bf16[512,768]{1,0:T(8,128)(2,1)S(1)} custom-call(bf16[512,768]{1,0:T(8,128)(2,1)} %tok_hbm.1, bf16[96,2304]{1,0:T(8,128)(2,1)} %wp_hbm.1, bf16[96,768]{1,0:T(8,128)(2,1)} %wo_hbm.1), custom_call_target="tpu_custom_call" | custom-call | tf_op jit(solution)/shard_map/pallas_call | solution.py:382
  46.8 1.5 %shard_map.38 = bf16[512,768]{1,0:T(8,128)(2,1)} custom-call(bf16[512,768]{1,0:T(8,128)(2,1)S(1)} %shard_map.37.y), custom_call_target="tpu_custom_call" | custom-call | tf_op jit(solution)/shard_map/pallas_call | solution.py:408

commit v6 on v5

--- a/solution.py
+++ b/solution.py
@@ -315,6 +315,8 @@
             for lo in range(2):
                 b = slice(32 * lo, 32 * lo + 32)
                 both[e, t, lo] = merge(first[e, t, lo], (pk[b], tot[b], num[b]))
+            o = [both[e, t, lo][2] / both[e, t, lo][1] for lo in range(2)]
+            att[e, 32 * t : 32 * t + 32, 128 * t : 128 * t + 128] = jnp.where(low, o[0], o[1]).astype(BF)
 
     outp.finish()
     for g in weights + (outp,):
@@ -347,8 +349,8 @@
             for lo in range(2):
                 pk, tot, num = both[e, t, lo]
                 _, tot8, num8 = merge((pk[:8], tot[:8], num[:8]), d)
-                o.append(jnp.concatenate([num8 / tot8, num[8:] / tot[8:]], axis=0))
-            att[e, 32 * t : 32 * t + 32, 128 * t : 128 * t + 128] = jnp.where(low, o[0], o[1]).astype(BF)
+                o.append(jnp.concatenate([num8 / tot8, num[8:16] / tot[8:16]], axis=0))
+            att[e, 32 * t : 32 * t + 16, 128 * t : 128 * t + 128] = jnp.where(low, o[0], o[1]).astype(BF)
 
     low384 = iota((1, 384), 1) % 128 < 64
 

time: 48.5 us -> 48.5 us (level)
  no operation moved by 1% of the time
where the time goes in v6:
time: 48.5 us; the launch traced here: 48.3 us
  Pallas kernels  48.3 us (100%)
    pallas_call x1, Pallas kernels, shards(): pl.pallas_call(kernel, out_shape=pltpu.VMEM((512, 768), BF), in_specs=[hb...  46.8 us
    pallas_call x1, Pallas kernels, shards(): pl.pallas_call(in_order, out_shape=jax.ShapeDtypeStruct((512, 768), BF),...  1.53 us

profile of v6, /device:TPU:1, one launch (start us, length us, event | category | flops | bytes accessed | tf_op | source)
XLA Modules:
  0.0 48.3 jit_solution(14391954743806921707)
XLA Ops:
  0.0 46.8 %shard_map.37.y = bf16[512,768]{1,0:T(8,128)(2,1)S(1)} custom-call(bf16[512,768]{1,0:T(8,128)(2,1)} %tok_hbm.1, bf16[96,2304]{1,0:T(8,128)(2,1)} %wp_hbm.1, bf16[96,768]{1,0:T(8,128)(2,1)} %wo_hbm.1), custom_call_target="tpu_custom_call" | custom-call | tf_op jit(solution)/shard_map/pallas_call | solution.py:384
  46.8 1.5 %shard_map.38 = bf16[512,768]{1,0:T(8,128)(2,1)} custom-call(bf16[512,768]{1,0:T(8,128)(2,1)S(1)} %shard_map.37.y), custom_call_target="tpu_custom_call" | custom-call | tf_op jit(solution)/shard_map/pallas_call | solution.py:410
